TPU v7x, 128 devices: a whole 4x4x4 slice. The times are simulated.
128 devices in a mesh: wide: 8 (over y, core), col: 16 (over z, x).
Axes of the slice: x: 4, y: 4, z: 4, core: 2. Of those that a mesh axis runs over, the one named last changes fastest.
Arguments:
- rhs: float32 [98304, 256], P(('wide', 'col')), may hold values from -6 to 6
- basis: bfloat16 [98304, 256], P(('wide', 'col')), may hold values from -0.21875 to 0.21875
- self_block: bfloat16 [98304, 768], P(('wide', 'col'))
- near_block: bfloat16 [128, 8, 768, 768], P(('wide', 'col')), may hold values from -0.0546875 to 0.0546875
- near_ids: int32 [128, 8], P(('wide', 'col')), may hold values from -1 to 127, as said below
- couplings: bfloat16 [128, 40, 256, 256], P(('wide', 'col')), may hold values from -0.09375 to 0.09375
- far_ids: int32 [128, 40], P(('wide', 'col')), may hold values from -1 to 127, as said below
- intersection_start: int32 [128, 2], P(('wide', 'col')), may hold values from 0 to 512
- schwarz_inverse: bfloat16 [128, 1280, 1280], P(('wide', 'col'))
Outputs:
- solution: float32 [98304, 256], P(('wide', 'col'))
Inputs may be any that keep to these rules, and one draw needn't show every extreme that they name: `near_ids`: row c lists every cluster adjacent to cluster c on the grid (larger index distance 1; id = first index * 16 + second), ids first and -1 after them; rows of corner and edge clusters end in -1. `far_ids`: row c lists distinct clusters whose larger grid index distance from cluster c is 2 to 3, ids first and -1 after them; counts are ragged, and some rows list every such cluster. `intersection_start`: column 0 starts the rows taken by the domain of the cluster before along the second grid index, column 1 those taken by the one after.
All inputs are finite; a program needn't handle non-finite values.
Results may differ from a plain program's by a relative error of at most 0.0025.
The roundings to bfloat16 on the way count: a program that leaves them out, or rounds other values in their place, can miss the bound.
Values may be sent and summed in bfloat16 or wider, within the bound.
A program may use at most 128 MiB of HBM per device.

v0:
```python
import jax
import jax.numpy as jnp
from jax import lax
from jax.sharding import PartitionSpec as P

REACH = 3
ITERS = 2
HIGHEST_PREC = lax.Precision.HIGHEST
GROUP_SLOTS = 8


def passed_along(block, axis, distance):
    devices = range(lax.axis_size(axis))
    route = [(i - distance, i) for i in devices if i - distance in devices]
    return lax.ppermute(block, axis, route)


def with_halo(block, sides, width):
    for axis, dim in sides:
        count = lax.axis_size(axis)
        forward = [(i, i + 1) for i in range(count - 1)]
        backward = [(target, source) for source, target in forward]
        low = lax.ppermute(
            lax.slice_in_dim(block, block.shape[dim] - width, None, axis=dim), axis, forward
        )
        high = lax.ppermute(lax.slice_in_dim(block, 0, width, axis=dim), axis, backward)
        block = jnp.concatenate([low, block, high], axis=dim)
    return block


def local_gram(left, right):
    return lax.dot_general(
        left,
        right,
        (((0,), (0,)), ((), ())),
        precision=HIGHEST_PREC,
        preferred_element_type=jnp.float32,
    )


def lower_solve(factor, matrix):
    return lax.linalg.triangular_solve(
        factor, matrix, left_side=False, lower=True, transpose_a=True
    )


def far_window(coefficients):
    strip_row = jnp.stack(
        [
            coefficients if offset == 0 else passed_along(coefficients, "col", -offset)
            for offset in range(-REACH, REACH + 1)
        ]
    )
    window = jnp.stack(
        [
            strip_row if offset == 0 else passed_along(strip_row, "wide", -offset)
            for offset in range(-REACH, REACH + 1)
        ]
    )
    return window


def operate(vector_in, basis, self_block, near_block, near_ids, couplings, far_ids):
    rounded = vector_in.astype(jnp.bfloat16)
    cluster_rows, width = rounded.shape
    rank = basis.shape[1]
    wide_pos = lax.axis_index("wide")
    col_pos = lax.axis_index("col")
    col_count = lax.axis_size("col")
    result = jnp.dot(self_block, rounded, preferred_element_type=jnp.float32)
    beside_all = with_halo(rounded[None, None], (("wide", 0), ("col", 1)), 1)
    for slot_index in range(near_ids.shape[1]):
        neighbour = near_ids[0, slot_index]
        safe_id = jnp.maximum(neighbour, 0)
        wide_off = safe_id // col_count - wide_pos + 1
        col_off = safe_id % col_count - col_pos + 1
        other = lax.dynamic_slice(
            beside_all, (wide_off, col_off, 0, 0), (1, 1, cluster_rows, width)
        )[0, 0]
        product = jnp.dot(near_block[0, slot_index], other, preferred_element_type=jnp.float32)
        result = result + jnp.where(neighbour >= 0, product, jnp.zeros_like(product))
    coefficients = lax.dot_general(
        basis, rounded, (((0,), (0,)), ((), ())), preferred_element_type=jnp.float32
    ).astype(jnp.bfloat16)
    window = far_window(coefficients)
    span = 2 * REACH + 1
    flat_window = window.reshape(span * span, rank, width)
    far_list = far_ids[0]
    live_count = jnp.sum((far_list >= 0).astype(jnp.int32))
    group_count = (live_count + GROUP_SLOTS - 1) // GROUP_SLOTS

    def add_group(group_index, running):
        first_slot = group_index * GROUP_SLOTS
        targets = lax.dynamic_slice_in_dim(far_list, first_slot, GROUP_SLOTS, 0)
        safe_ids = jnp.maximum(targets, 0)
        flat_index = (safe_ids // col_count - wide_pos + REACH) * span + (
            safe_ids % col_count - col_pos + REACH
        )
        pieces_in = jnp.take(flat_window, flat_index, axis=0)
        coupling_group = lax.dynamic_slice_in_dim(couplings[0], first_slot, GROUP_SLOTS, 0)
        live_slots = (targets >= 0)[:, None, None]
        coupling_group = jnp.where(live_slots, coupling_group, jnp.zeros_like(coupling_group))
        return running + jnp.einsum(
            "lrs,lsk->rk", coupling_group, pieces_in, preferred_element_type=jnp.float32
        )

    far_sum = lax.fori_loop(0, group_count, add_group, jnp.zeros((rank, width), jnp.float32))
    return result + jnp.dot(basis, far_sum.astype(jnp.bfloat16), preferred_element_type=jnp.float32)


def add_rows(matrix, addend, start):
    current = lax.dynamic_slice_in_dim(matrix, start, addend.shape[0], 0)
    return lax.dynamic_update_slice_in_dim(matrix, current + addend, start, 0)


def precondition(vector_in, intersection_start, schwarz_inverse):
    rounded = vector_in.astype(jnp.bfloat16)
    cluster_rows = rounded.shape[0]
    margin = (schwarz_inverse.shape[1] - cluster_rows) // 2
    starts = intersection_start[0]
    prev_whole, prev_starts = passed_along((rounded, intersection_start), "col", 1)
    next_whole, next_starts = passed_along((rounded, intersection_start), "col", -1)
    prev_rows = lax.dynamic_slice_in_dim(prev_whole, prev_starts[0, 1], margin, 0)
    next_rows = lax.dynamic_slice_in_dim(next_whole, next_starts[0, 0], margin, 0)
    domain = jnp.concatenate([prev_rows, rounded, next_rows], axis=0)
    solved = jnp.dot(schwarz_inverse[0], domain, preferred_element_type=jnp.float32)
    result = solved[margin : margin + cluster_rows]
    from_next = passed_along(solved[:margin], "col", -1)
    from_prev = passed_along(solved[margin + cluster_rows :], "col", 1)
    result = add_rows(result, from_next, starts[1])
    result = add_rows(result, from_prev, starts[0])
    return result


def on_device(
    rhs,
    basis,
    self_block,
    near_block,
    near_ids,
    couplings,
    far_ids,
    intersection_start,
    schwarz_inverse,
):
    width = rhs.shape[1]
    first_sum = lax.psum(local_gram(rhs, rhs), ("wide", "col"))
    factor = jnp.linalg.cholesky(first_sum)
    beta_block = factor.T
    bases = [lower_solve(factor, rhs)]
    directions = []
    columns = []
    for iteration in range(ITERS):
        precond_out = precondition(bases[-1], intersection_start, schwarz_inverse)
        image = operate(precond_out, basis, self_block, near_block, near_ids, couplings, far_ids)
        stacked = jnp.concatenate(bases, axis=1)
        projected = lax.psum(local_gram(stacked, image), ("wide", "col"))
        image = image - jnp.dot(stacked, projected, precision=HIGHEST_PREC)
        gram_sum = lax.psum(local_gram(image, image), ("wide", "col"))
        factor = jnp.linalg.cholesky(gram_sum)
        columns.append((projected, factor.T))
        directions.append(precond_out)
        if iteration + 1 < ITERS:
            bases.append(lower_solve(factor, image))
    hessen = jnp.zeros(((ITERS + 1) * width, ITERS * width), jnp.float32)
    for column_index, (projected, sub_block) in enumerate(columns):
        upper_rows = (column_index + 1) * width
        hessen = hessen.at[:upper_rows, column_index * width : (column_index + 1) * width].set(
            projected
        )
        hessen = hessen.at[
            upper_rows : upper_rows + width, column_index * width : (column_index + 1) * width
        ].set(sub_block)
    normal_matrix = jnp.dot(hessen.T, hessen, precision=HIGHEST_PREC)
    target = jnp.dot(hessen[:width].T, beta_block, precision=HIGHEST_PREC)
    small_factor = jnp.linalg.cholesky(normal_matrix)
    middle = lax.linalg.triangular_solve(small_factor, target, left_side=True, lower=True)
    weights_y = lax.linalg.triangular_solve(
        small_factor, middle, left_side=True, lower=True, transpose_a=True
    )
    return jnp.dot(jnp.concatenate(directions, axis=1), weights_y, precision=HIGHEST_PREC)


def solution(mesh):
    in_specs = (
        P(("wide", "col"), None),
        P(("wide", "col"), None),
        P(("wide", "col"), None),
        P(("wide", "col"), None, None, None),
        P(("wide", "col"), None),
        P(("wide", "col"), None, None, None),
        P(("wide", "col"), None),
        P(("wide", "col"), None),
        P(("wide", "col"), None, None),
    )
    out_specs = P(("wide", "col"), None)
    return jax.shard_map(
        on_device, mesh=mesh, in_specs=in_specs, out_specs=out_specs, check_vma=False
    )
```

profile of v0, /device:TPU:1, one launch (start us, length us, event | category | flops | bytes accessed | tf_op | source)
XLA Modules:
  0.0 1556.4 jit_solution(12817224653365156530)
XLA Ops:
  10.3 146.7 %all-reduce.9.cloned.1.call-done = f32[256,256]{0,1:T(8,128)} async-done(((f32[256,256]{0,1:T(8,128)}), f32[256,256]{0,1:T(8,128)}) %all-reduce.9.cloned.1.call-update) | async-done | bytes 262160 | tf_op jit(solution)/shard_map/psum | solution.py:147
  159.7 11.7 cholesky.392
  186.2 13.2 cholesky.402
  211.1 21.1 %custom-call.48 = f32[2,128,128]{1,2,0:T(8,128)} custom-call(f32[2,128,128]{2,1,0:T(8,128)} %get-tuple-element.295), custom_call_target="InvertDiagBlocksLowerTriangular" | custom-call | tf_op jit(solution)/shard_map/triangular_solve/custom-call.9 | solution.py:42
  339.1 19.0 %collective-permute-done.6 = bf16[1,1,768,256]{2,3,1,0:T(8,128)(2,1)} collective-permute-done((bf16[1,1,768,256]{2,3,1,0:T(8,128)(2,1)}, bf16[1,1,768,256]{2,3,1,0:T(8,128)(2,1)}, u32[]{:S(2)}, u32[]{:S(2)}) %collective-permute-start.6) | collective-permute-done | bytes 393248 | tf_op jit(solution)/shard_map/ppermute | solution.py:23
  397.9 14.7 while.33
  428.6 185.3 %all-reduce.11.cloned.1.call-done = f32[256,256]{1,0:T(8,128)} async-done(((f32[256,256]{1,0:T(8,128)}), f32[256,256]{1,0:T(8,128)}) %all-reduce.11.cloned.1.call-update) | async-done | bytes 262160 | tf_op jit(solution)/shard_map/psum | solution.py:157
  618.9 138.9 %all-reduce.13.cloned.1.call-done = f32[256,256]{0,1:T(8,128)} async-done(((f32[256,256]{0,1:T(8,128)}), f32[256,256]{0,1:T(8,128)}) %all-reduce.13.cloned.1.call-update) | async-done | bytes 262160 | tf_op jit(solution)/shard_map/psum | solution.py:159
  762.0 13.2 cholesky.419
  778.2 11.3 custom-call.49
  792.9 13.2 cholesky.429
  820.2 21.1 %custom-call.50 = f32[2,128,128]{1,2,0:T(8,128)} custom-call(f32[2,128,128]{2,1,0:T(8,128)} %get-tuple-element.296), custom_call_target="InvertDiagBlocksLowerTriangular" | custom-call | tf_op jit(solution)/shard_map/triangular_solve/custom-call.9 | solution.py:42
  922.9 30.5 %collective-permute-done.26 = bf16[1,1,768,256]{2,3,1,0:T(8,128)(2,1)S(1)} collective-permute-done((bf16[1,1,768,256]{2,3,1,0:T(8,128)(2,1)S(1)}, bf16[1,1,768,256]{2,3,1,0:T(8,128)(2,1)S(1)}, u32[]{:S(2)}, u32[]{:S(2)}) %collective-permute-start.26) | collective-permute-done | bytes 393248 | tf_op jit(solution)/shard_map/ppermute | solution.py:23
  993.1 12.1 while.34
  1023.1 184.5 %all-reduce.15.cloned.1.call-done = f32[512,256]{1,0:T(8,128)} async-done(((f32[512,256]{1,0:T(8,128)}), f32[512,256]{1,0:T(8,128)}) %all-reduce.15.cloned.1.call-update) | async-done | bytes 524304 | tf_op jit(solution)/shard_map/psum | solution.py:157
  1221.8 131.3 %all-reduce.17.cloned.1.call-done = f32[256,256]{0,1:T(8,128)} async-done(((f32[256,256]{0,1:T(8,128)}), f32[256,256]{0,1:T(8,128)}) %all-reduce.17.cloned.1.call-update) | async-done | bytes 262160 | tf_op jit(solution)/shard_map/psum | solution.py:159
  1355.2 11.7 cholesky.446
  1377.2 11.7 cholesky.456
  1397.7 11.7 cholesky.167
  1421.9 11.9 cholesky.190
  1446.5 11.7 cholesky.294
  1470.2 11.9 cholesky.307
  1485.6 10.6 while.35
  1496.2 40.2 %custom-call.39 = f32[4,128,128]{1,2,0:T(8,128)S(1)} custom-call(f32[4,128,128]{2,1,0:T(8,128)} %get-tuple-element.288), custom_call_target="InvertDiagBlocksLowerTriangular" | custom-call | tf_op jit(solution)/shard_map/triangular_solve | solution.py:178
  (415 shorter events, 480.9 us)
Async XLA Ops:
  6.5 150.4 %all-reduce.9.cloned.1.call-start = ((), (), s32[]{:S(2)}) async-start(), calls=%async_computation | async-start | bytes 524288 | tf_op jit(solution)/shard_map/psum | solution.py:147
  10.2 603.7 %all-reduce.11.cloned.1.call-start = ((), (), s32[]{:S(2)}) async-start(), calls=%async_computation.1 | async-start | bytes 524288 | tf_op jit(solution)/shard_map/psum | solution.py:157
  309.5 54.3 %collective-permute-start.16 = (bf16[7,256,256]{1,2,0:T(8,128)(2,1)}, bf16[7,256,256]{1,2,0:T(8,128)(2,1)}, u32[]{:S(2)}, u32[]{:S(2)}) collective-permute-start(bf16[7,256,256]{1,2,0:T(8,128)(2,1)} %bitcast_dynamic-update-slice_fusion.25), channel_id=1, source_target_pairs={{0,48},{16,64},{32,80},{48,96},{64,112},{1,49},{17,65},{33,81},{49... | collective-permute-start | bytes 2752520 | tf_op jit(solution)/shard_map/ppermute | solution.py:15
  316.5 50.7 %collective-permute-start.17 = (bf16[7,256,256]{1,2,0:T(8,128)(2,1)}, bf16[7,256,256]{1,2,0:T(8,128)(2,1)}, u32[]{:S(2)}, u32[]{:S(2)}) collective-permute-start(bf16[7,256,256]{1,2,0:T(8,128)(2,1)} %bitcast_dynamic-update-slice_fusion.25), channel_id=1, source_target_pairs={{0,32},{16,48},{32,64},{48,80},{64,96},{80,112},{1,33},{17,49},{33... | collective-permute-start | bytes 2752520 | tf_op jit(solution)/shard_map/ppermute | solution.py:15
  319.5 38.6 %collective-permute-start.6 = (bf16[1,1,768,256]{2,3,1,0:T(8,128)(2,1)}, bf16[1,1,768,256]{2,3,1,0:T(8,128)(2,1)}, u32[]{:S(2)}, u32[]{:S(2)}) collective-permute-start(bf16[1,1,768,256]{2,3,1,0:T(8,128)(2,1)} %convert_bitcast_fusion.1), channel_id=1, source_target_pairs={{0,16},{16,32},{32,48},{48,64},{64,80},{80,96},{96,112},{1,17},{17... | collective-permute-start | bytes 1179656 | tf_op jit(solution)/shard_map/ppermute | solution.py:23
  321.5 38.6 %collective-permute-start.7 = (bf16[1,1,768,256]{2,3,1,0:T(8,128)(2,1)}, bf16[1,1,768,256]{2,3,1,0:T(8,128)(2,1)}, u32[]{:S(2)}, u32[]{:S(2)}) collective-permute-start(bf16[1,1,768,256]{2,3,1,0:T(8,128)(2,1)} %convert_bitcast_fusion.1), channel_id=1, source_target_pairs={{16,0},{32,16},{48,32},{64,48},{80,64},{96,80},{112,96},{17,1},{33... | collective-permute-start | bytes 1179656 | tf_op jit(solution)/shard_map/ppermute | solution.py:26
  324.6 49.8 %collective-permute-start.18 = (bf16[7,256,256]{1,2,0:T(8,128)(2,1)}, bf16[7,256,256]{1,2,0:T(8,128)(2,1)}, u32[]{:S(2)}, u32[]{:S(2)}) collective-permute-start(bf16[7,256,256]{1,2,0:T(8,128)(2,1)} %bitcast_dynamic-update-slice_fusion.25), channel_id=1, source_target_pairs={{0,16},{16,32},{32,48},{48,64},{64,80},{80,96},{96,112},{1,17},{17... | collective-permute-start | bytes 2752520 | tf_op jit(solution)/shard_map/ppermute | solution.py:15
  358.2 23.7 %collective-permute-start.19 = (bf16[7,256,256]{1,2,0:T(8,128)(2,1)}, bf16[7,256,256]{1,2,0:T(8,128)(2,1)S(1)}, u32[]{:S(2)}, u32[]{:S(2)}) collective-permute-start(bf16[7,256,256]{1,2,0:T(8,128)(2,1)} %bitcast_dynamic-update-slice_fusion.25), channel_id=1, source_target_pairs={{16,0},{32,16},{48,32},{64,48},{80,64},{96,80},{112,96},{17,1},{33... | collective-permute-start | bytes 2752520 | tf_op jit(solution)/shard_map/ppermute | solution.py:15
  360.1 25.7 %collective-permute-start.20 = (bf16[7,256,256]{1,2,0:T(8,128)(2,1)}, bf16[7,256,256]{1,2,0:T(8,128)(2,1)S(1)}, u32[]{:S(2)}, u32[]{:S(2)}) collective-permute-start(bf16[7,256,256]{1,2,0:T(8,128)(2,1)} %bitcast_dynamic-update-slice_fusion.25), channel_id=1, source_target_pairs={{32,0},{48,16},{64,32},{80,48},{96,64},{112,80},{33,1},{49,17},{65... | collective-permute-start | bytes 2752520 | tf_op jit(solution)/shard_map/ppermute | solution.py:15
  367.2 45.4 %collective-permute-start.8 = (bf16[3,1,768,256]{2,3,1,0:T(8,128)(2,1)}, bf16[3,1,768,256]{2,3,1,0:T(8,128)(2,1)}, u32[]{:S(2)}, u32[]{:S(2)}) collective-permute-start(bf16[3,1,768,256]{2,3,1,0:T(8,128)(2,1)} %pad_maximum_fusion.2), channel_id=1, source_target_pairs={{0,1},{1,2},{2,3},{3,4},{4,5},{5,6},{6,7},{7,8},{8,9},{9,10},{10,1... | collective-permute-start | bytes 3538952 | tf_op jit(solution)/shard_map/ppermute | solution.py:23
  374.4 38.2 %collective-permute-start.9 = (bf16[3,1,768,256]{2,3,1,0:T(8,128)(2,1)}, bf16[3,1,768,256]{2,3,1,0:T(8,128)(2,1)}, u32[]{:S(2)}, u32[]{:S(2)}) collective-permute-start(bf16[3,1,768,256]{2,3,1,0:T(8,128)(2,1)} %pad_maximum_fusion.2), channel_id=1, source_target_pairs={{1,0},{2,1},{3,2},{4,3},{5,4},{6,5},{7,6},{8,7},{9,8},{10,9},{11,1... | collective-permute-start | bytes 3538952 | tf_op jit(solution)/shard_map/ppermute | solution.py:26
  428.5 329.3 %all-reduce.13.cloned.1.call-start = ((), (), s32[]{:S(2)}) async-start(), calls=%async_computation.2 | async-start | bytes 524288 | tf_op jit(solution)/shard_map/psum | solution.py:159
  618.6 589.0 %all-reduce.15.cloned.1.call-start = ((), (), s32[]{:S(2)}) async-start(), calls=%async_computation.3 | async-start | bytes 1048576 | tf_op jit(solution)/shard_map/psum | solution.py:157
  904.8 52.9 %collective-permute-start.36 = (bf16[7,256,256]{1,2,0:T(8,128)(2,1)}, bf16[7,256,256]{1,2,0:T(8,128)(2,1)}, u32[]{:S(2)}, u32[]{:S(2)}) collective-permute-start(bf16[7,256,256]{1,2,0:T(8,128)(2,1)} %bitcast_dynamic-update-slice_fusion.19), channel_id=1, source_target_pairs={{0,48},{16,64},{32,80},{48,96},{64,112},{1,49},{17,65},{33,81},{49... | collective-permute-start | bytes 2752520 | tf_op jit(solution)/shard_map/ppermute | solution.py:15
  913.1 48.1 %collective-permute-start.37 = (bf16[7,256,256]{1,2,0:T(8,128)(2,1)}, bf16[7,256,256]{1,2,0:T(8,128)(2,1)}, u32[]{:S(2)}, u32[]{:S(2)}) collective-permute-start(bf16[7,256,256]{1,2,0:T(8,128)(2,1)} %bitcast_dynamic-update-slice_fusion.19), channel_id=1, source_target_pairs={{0,32},{16,48},{32,64},{48,80},{64,96},{80,112},{1,33},{17,49},{33... | collective-permute-start | bytes 2752520 | tf_op jit(solution)/shard_map/ppermute | solution.py:15
  915.3 38.0 %collective-permute-start.26 = (bf16[1,1,768,256]{2,3,1,0:T(8,128)(2,1)S(1)}, bf16[1,1,768,256]{2,3,1,0:T(8,128)(2,1)S(1)}, u32[]{:S(2)}, u32[]{:S(2)}) collective-permute-start(bf16[1,1,768,256]{2,3,1,0:T(8,128)(2,1)S(1)} %convert_bitcast_fusion), channel_id=1, source_target_pairs={{0,16},{16,32},{32,48},{48,64},{64,80},{80,96},{96,112},{1,17},{17... | collective-permute-start | bytes 1179656 | tf_op jit(solution)/shard_map/ppermute | solution.py:23
  917.3 38.0 %collective-permute-start.27 = (bf16[1,1,768,256]{2,3,1,0:T(8,128)(2,1)S(1)}, bf16[1,1,768,256]{2,3,1,0:T(8,128)(2,1)S(1)}, u32[]{:S(2)}, u32[]{:S(2)}) collective-permute-start(bf16[1,1,768,256]{2,3,1,0:T(8,128)(2,1)S(1)} %convert_bitcast_fusion), channel_id=1, source_target_pairs={{16,0},{32,16},{48,32},{64,48},{80,64},{96,80},{112,96},{17,1},{33... | collective-permute-start | bytes 1179656 | tf_op jit(solution)/shard_map/ppermute | solution.py:26
  919.7 48.7 %collective-permute-start.38 = (bf16[7,256,256]{1,2,0:T(8,128)(2,1)}, bf16[7,256,256]{1,2,0:T(8,128)(2,1)}, u32[]{:S(2)}, u32[]{:S(2)}) collective-permute-start(bf16[7,256,256]{1,2,0:T(8,128)(2,1)} %bitcast_dynamic-update-slice_fusion.19), channel_id=1, source_target_pairs={{0,16},{16,32},{32,48},{48,64},{64,80},{80,96},{96,112},{1,17},{17... | collective-permute-start | bytes 2752520 | tf_op jit(solution)/shard_map/ppermute | solution.py:15
  953.3 23.7 %collective-permute-start.39 = (bf16[7,256,256]{1,2,0:T(8,128)(2,1)}, bf16[7,256,256]{1,2,0:T(8,128)(2,1)S(1)}, u32[]{:S(2)}, u32[]{:S(2)}) collective-permute-start(bf16[7,256,256]{1,2,0:T(8,128)(2,1)} %bitcast_dynamic-update-slice_fusion.19), channel_id=1, source_target_pairs={{16,0},{32,16},{48,32},{64,48},{80,64},{96,80},{112,96},{17,1},{33... | collective-permute-start | bytes 2752520 | tf_op jit(solution)/shard_map/ppermute | solution.py:15
  955.3 25.7 %collective-permute-start.40 = (bf16[7,256,256]{1,2,0:T(8,128)(2,1)}, bf16[7,256,256]{1,2,0:T(8,128)(2,1)S(1)}, u32[]{:S(2)}, u32[]{:S(2)}) collective-permute-start(bf16[7,256,256]{1,2,0:T(8,128)(2,1)} %bitcast_dynamic-update-slice_fusion.19), channel_id=1, source_target_pairs={{32,0},{48,16},{64,32},{80,48},{96,64},{112,80},{33,1},{49,17},{65... | collective-permute-start | bytes 2752520 | tf_op jit(solution)/shard_map/ppermute | solution.py:15
  957.7 24.2 %collective-permute-start.41 = (bf16[7,256,256]{1,2,0:T(8,128)(2,1)}, bf16[7,256,256]{1,2,0:T(8,128)(2,1)S(1)}, u32[]{:S(2)}, u32[]{:S(2)}) collective-permute-start(bf16[7,256,256]{1,2,0:T(8,128)(2,1)} %bitcast_dynamic-update-slice_fusion.19), channel_id=1, source_target_pairs={{48,0},{64,16},{80,32},{96,48},{112,64},{49,1},{65,17},{81,33},{97... | collective-permute-start | bytes 2752520 | tf_op jit(solution)/shard_map/ppermute | solution.py:15
  961.2 44.0 %collective-permute-start.28 = (bf16[3,1,768,256]{2,3,1,0:T(8,128)(2,1)}, bf16[3,1,768,256]{2,3,1,0:T(8,128)(2,1)}, u32[]{:S(2)}, u32[]{:S(2)}) collective-permute-start(bf16[3,1,768,256]{2,3,1,0:T(8,128)(2,1)} %pad_maximum_fusion.3), channel_id=1, source_target_pairs={{0,1},{1,2},{2,3},{3,4},{4,5},{5,6},{6,7},{7,8},{8,9},{9,10},{10,1... | collective-permute-start | bytes 3538952 | tf_op jit(solution)/shard_map/ppermute | solution.py:23
  968.4 36.7 %collective-permute-start.29 = (bf16[3,1,768,256]{2,3,1,0:T(8,128)(2,1)}, bf16[3,1,768,256]{2,3,1,0:T(8,128)(2,1)}, u32[]{:S(2)}, u32[]{:S(2)}) collective-permute-start(bf16[3,1,768,256]{2,3,1,0:T(8,128)(2,1)} %pad_maximum_fusion.3), channel_id=1, source_target_pairs={{1,0},{2,1},{3,2},{4,3},{5,4},{6,5},{7,6},{8,7},{9,8},{10,9},{11,1... | collective-permute-start | bytes 3538952 | tf_op jit(solution)/shard_map/ppermute | solution.py:26
  1020.4 332.6 %all-reduce.17.cloned.1.call-start = ((), (), s32[]{:S(2)}) async-start(), calls=%async_computation.4 | async-start | bytes 524288 | tf_op jit(solution)/shard_map/psum | solution.py:159
  (68 other events, 1608.7 us)
Sparse Core Ops, SparseCore 0:
  12.1 144.7 all-reduce.8
  428.6 185.2 all-reduce.10
  618.8 138.9 all-reduce.12
  1020.6 186.9 all-reduce.14
  1212.9 140.1 all-reduce.16
where the time goes:
time: 1570 us; the launch traced here: 1560 us
  waiting for transfers between devices  876 us (56%)
  other arithmetic  300 us (19%)
  local copies, waits for them, and re-layouts  133 us (8%)
  starting transfers between devices  117 us (7%)
  matrix products  91.5 us (6%)
  between operations  37.7 us (2%)
    psum x2, waiting for transfers between devices, on_device(): projected = lax.psum(local_gram(stacked, image), ('wide', 'col'))  370 us
    psum x2, waiting for transfers between devices, on_device(): gram_sum = lax.psum(local_gram(image, image), ('wide', 'col'))  270 us
    psum x1, waiting for transfers between devices, on_device(): first_sum = lax.psum(local_gram(rhs, rhs), ('wide', 'col'))  147 us
    ppermute x34, starting transfers between devices, passed_along(): return lax.ppermute(block, axis, route)  94.5 us
    another operation x15, other arithmetic, on_device(): small_factor = jnp.linalg.cholesky(normal_matrix)  79.5 us
    another operation x14, other arithmetic, on_device(): factor = jnp.linalg.cholesky(gram_sum)  76.6 us
    ppermute x4, waiting for transfers between devices, with_halo(): lax.ppermute(lax.slice_in_dim(block, block.shape[dim] - width, None, axis...  49.5 us
    another operation x4, other arithmetic, lower_solve(): lax.linalg.triangular_solve(factor, matrix, left_side=False, lower=True,...  42.9 us
  transfers between devices with their start and end apart: 47, of which 22 were waited for; matrix products, arithmetic and copies ran while one was open for 7% of the time, Pallas kernels for 0%

commit v1 on v0

--- a/solution.py
+++ b/solution.py
@@ -154,7 +154,7 @@
         precond_out = precondition(bases[-1], intersection_start, schwarz_inverse)
         image = operate(precond_out, basis, self_block, near_block, near_ids, couplings, far_ids)
         stacked = jnp.concatenate(bases, axis=1)
-        projected = lax.psum(local_gram(stacked, image), ("wide", "col"))
+        projected = lax.psum(lax.psum(local_gram(stacked, image), "wide"), "col")
         image = image - jnp.dot(stacked, projected, precision=HIGHEST_PREC)
         gram_sum = lax.psum(local_gram(image, image), ("wide", "col"))
         factor = jnp.linalg.cholesky(gram_sum)

time: 1570 us -> 1580 us (level)
    psum x2 -> x4, waiting for transfers between devices: 370 us -> 376 us  [on_device(): projected = lax.psum(lax.psum(local_gram(stacked, image), 'wide'), 'col')]
  transfers between devices with their start and end apart: 47 -> 49, of which waited for: 22 -> 24; matrix products, arithmetic and copies ran while one was open for 7% -> 7% of each run, Pallas kernels for 0% -> 0%
where the time goes in v1:
time: 1580 us; the launch traced here: 1570 us
  waiting for transfers between devices  886 us (56%)
  other arithmetic  300 us (19%)
  local copies, waits for them, and re-layouts  133 us (8%)
  starting transfers between devices  117 us (7%)
  matrix products  91.5 us (6%)
  between operations  38.1 us (2%)
    psum x4, waiting for transfers between devices, on_device(): projected = lax.psum(lax.psum(local_gram(stacked, image), 'wide'), 'col')  376 us
    psum x2, waiting for transfers between devices, on_device(): gram_sum = lax.psum(local_gram(image, image), ('wide', 'col'))  275 us
    psum x1, waiting for transfers between devices, on_device(): first_sum = lax.psum(local_gram(rhs, rhs), ('wide', 'col'))  147 us
    ppermute x34, starting transfers between devices, passed_along(): return lax.ppermute(block, axis, route)  94.5 us
    another operation x15, other arithmetic, on_device(): small_factor = jnp.linalg.cholesky(normal_matrix)  79.5 us
    another operation x14, other arithmetic, on_device(): factor = jnp.linalg.cholesky(gram_sum)  76.6 us
    ppermute x4, waiting for transfers between devices, with_halo(): lax.ppermute(lax.slice_in_dim(block, block.shape[dim] - width, None, axis...  49.5 us
    another operation x4, other arithmetic, lower_solve(): lax.linalg.triangular_solve(factor, matrix, left_side=False, lower=True,...  42.9 us
  transfers between devices with their start and end apart: 49, of which 24 were waited for; matrix products, arithmetic and copies ran while one was open for 7% of the time, Pallas kernels for 0%

profile of v1, /device:TPU:1, one launch (start us, length us, event | category | flops | bytes accessed | tf_op | source)
XLA Modules:
  0.0 1567.3 jit_solution(7804689092650001579)
XLA Ops:
  10.3 146.7 %all-reduce.11.cloned.1.call-done = f32[256,256]{0,1:T(8,128)} async-done(((f32[256,256]{0,1:T(8,128)}), f32[256,256]{0,1:T(8,128)}) %all-reduce.11.cloned.1.call-update) | async-done | bytes 262160 | tf_op jit(solution)/shard_map/psum | solution.py:147
  159.7 11.7 cholesky.392
  186.2 13.2 cholesky.402
  211.1 21.1 %custom-call.48 = f32[2,128,128]{1,2,0:T(8,128)} custom-call(f32[2,128,128]{2,1,0:T(8,128)} %get-tuple-element.295), custom_call_target="InvertDiagBlocksLowerTriangular" | custom-call | tf_op jit(solution)/shard_map/triangular_solve/custom-call.9 | solution.py:42
  339.1 19.0 %collective-permute-done.6 = bf16[1,1,768,256]{2,3,1,0:T(8,128)(2,1)} collective-permute-done((bf16[1,1,768,256]{2,3,1,0:T(8,128)(2,1)}, bf16[1,1,768,256]{2,3,1,0:T(8,128)(2,1)}, u32[]{:S(2)}, u32[]{:S(2)}) %collective-permute-start.6) | collective-permute-done | bytes 393248 | tf_op jit(solution)/shard_map/ppermute | solution.py:23
  397.9 14.7 while.33
  428.5 101.6 %all-reduce.13.cloned.1.call-done = f32[256,256]{1,0:T(8,128)} async-done(((f32[256,256]{1,0:T(8,128)}), f32[256,256]{1,0:T(8,128)}) %all-reduce.13.cloned.1.call-update) | async-done | bytes 262160 | tf_op jit(solution)/shard_map/psum | solution.py:157
  530.2 87.7 %all-reduce.15.cloned.1.call-done = f32[256,256]{1,0:T(8,128)} async-done(((f32[256,256]{1,0:T(8,128)}), f32[256,256]{1,0:T(8,128)}) %all-reduce.15.cloned.1.call-update) | async-done | bytes 262160 | tf_op jit(solution)/shard_map/psum | solution.py:157
  622.9 142.0 %all-reduce.17.cloned.1.call-done = f32[256,256]{0,1:T(8,128)} async-done(((f32[256,256]{0,1:T(8,128)}), f32[256,256]{0,1:T(8,128)}) %all-reduce.17.cloned.1.call-update) | async-done | bytes 262160 | tf_op jit(solution)/shard_map/psum | solution.py:159
  769.1 13.2 cholesky.419
  800.1 13.2 cholesky.429
  827.3 21.1 %custom-call.50 = f32[2,128,128]{1,2,0:T(8,128)} custom-call(f32[2,128,128]{2,1,0:T(8,128)} %get-tuple-element.296), custom_call_target="InvertDiagBlocksLowerTriangular" | custom-call | tf_op jit(solution)/shard_map/triangular_solve/custom-call.9 | solution.py:42
  930.0 30.5 %collective-permute-done.26 = bf16[1,1,768,256]{2,3,1,0:T(8,128)(2,1)S(1)} collective-permute-done((bf16[1,1,768,256]{2,3,1,0:T(8,128)(2,1)S(1)}, bf16[1,1,768,256]{2,3,1,0:T(8,128)(2,1)S(1)}, u32[]{:S(2)}, u32[]{:S(2)}) %collective-permute-start.26) | collective-permute-done | bytes 393248 | tf_op jit(solution)/shard_map/ppermute | solution.py:23
  1000.2 12.1 while.34
  1027.6 100.5 %all-reduce.19.cloned.1.call-done = f32[512,256]{1,0:T(8,128)} async-done(((f32[512,256]{1,0:T(8,128)}), f32[512,256]{1,0:T(8,128)}) %all-reduce.19.cloned.1.call-update) | async-done | bytes 524304 | tf_op jit(solution)/shard_map/psum | solution.py:157
  1130.8 85.9 %all-reduce.21.cloned.1.call-done = f32[512,256]{1,0:T(8,128)} async-done(((f32[512,256]{1,0:T(8,128)}), f32[512,256]{1,0:T(8,128)}) %all-reduce.21.cloned.1.call-update) | async-done | bytes 524304 | tf_op jit(solution)/shard_map/psum | solution.py:157
  1230.9 132.8 %all-reduce.23.cloned.1.call-done = f32[256,256]{0,1:T(8,128)} async-done(((f32[256,256]{0,1:T(8,128)}), f32[256,256]{0,1:T(8,128)}) %all-reduce.23.cloned.1.call-update) | async-done | bytes 262160 | tf_op jit(solution)/shard_map/psum | solution.py:159
  1365.8 11.7 cholesky.446
  1387.9 11.7 cholesky.456
  1408.3 11.7 cholesky.167
  1432.5 11.9 cholesky.190
  1457.1 11.7 cholesky.294
  1480.9 11.9 cholesky.307
  1506.8 40.2 %custom-call.39 = f32[4,128,128]{1,2,0:T(8,128)S(1)} custom-call(f32[4,128,128]{2,1,0:T(8,128)} %get-tuple-element.288), custom_call_target="InvertDiagBlocksLowerTriangular" | custom-call | tf_op jit(solution)/shard_map/triangular_solve | solution.py:178
  (421 shorter events, 502.9 us)
Async XLA Ops:
  6.5 150.4 %all-reduce.11.cloned.1.call-start = ((), (), s32[]{:S(2)}) async-start(), calls=%async_computation | async-start | bytes 524288 | tf_op jit(solution)/shard_map/psum | solution.py:147
  10.2 519.9 %all-reduce.13.cloned.1.call-start = ((), (), s32[]{:S(2)}) async-start(), calls=%async_computation.1 | async-start | bytes 524288 | tf_op jit(solution)/shard_map/psum | solution.py:157
  309.4 54.3 %collective-permute-start.16 = (bf16[7,256,256]{1,2,0:T(8,128)(2,1)}, bf16[7,256,256]{1,2,0:T(8,128)(2,1)}, u32[]{:S(2)}, u32[]{:S(2)}) collective-permute-start(bf16[7,256,256]{1,2,0:T(8,128)(2,1)} %bitcast_dynamic-update-slice_fusion.25), channel_id=1, source_target_pairs={{0,48},{16,64},{32,80},{48,96},{64,112},{1,49},{17,65},{33,81},{49... | collective-permute-start | bytes 2752520 | tf_op jit(solution)/shard_map/ppermute | solution.py:15
  316.5 50.7 %collective-permute-start.17 = (bf16[7,256,256]{1,2,0:T(8,128)(2,1)}, bf16[7,256,256]{1,2,0:T(8,128)(2,1)}, u32[]{:S(2)}, u32[]{:S(2)}) collective-permute-start(bf16[7,256,256]{1,2,0:T(8,128)(2,1)} %bitcast_dynamic-update-slice_fusion.25), channel_id=1, source_target_pairs={{0,32},{16,48},{32,64},{48,80},{64,96},{80,112},{1,33},{17,49},{33... | collective-permute-start | bytes 2752520 | tf_op jit(solution)/shard_map/ppermute | solution.py:15
  319.5 38.6 %collective-permute-start.6 = (bf16[1,1,768,256]{2,3,1,0:T(8,128)(2,1)}, bf16[1,1,768,256]{2,3,1,0:T(8,128)(2,1)}, u32[]{:S(2)}, u32[]{:S(2)}) collective-permute-start(bf16[1,1,768,256]{2,3,1,0:T(8,128)(2,1)} %convert_bitcast_fusion.1), channel_id=1, source_target_pairs={{0,16},{16,32},{32,48},{48,64},{64,80},{80,96},{96,112},{1,17},{17... | collective-permute-start | bytes 1179656 | tf_op jit(solution)/shard_map/ppermute | solution.py:23
  321.5 38.6 %collective-permute-start.7 = (bf16[1,1,768,256]{2,3,1,0:T(8,128)(2,1)}, bf16[1,1,768,256]{2,3,1,0:T(8,128)(2,1)}, u32[]{:S(2)}, u32[]{:S(2)}) collective-permute-start(bf16[1,1,768,256]{2,3,1,0:T(8,128)(2,1)} %convert_bitcast_fusion.1), channel_id=1, source_target_pairs={{16,0},{32,16},{48,32},{64,48},{80,64},{96,80},{112,96},{17,1},{33... | collective-permute-start | bytes 1179656 | tf_op jit(solution)/shard_map/ppermute | solution.py:26
  324.6 49.8 %collective-permute-start.18 = (bf16[7,256,256]{1,2,0:T(8,128)(2,1)}, bf16[7,256,256]{1,2,0:T(8,128)(2,1)}, u32[]{:S(2)}, u32[]{:S(2)}) collective-permute-start(bf16[7,256,256]{1,2,0:T(8,128)(2,1)} %bitcast_dynamic-update-slice_fusion.25), channel_id=1, source_target_pairs={{0,16},{16,32},{32,48},{48,64},{64,80},{80,96},{96,112},{1,17},{17... | collective-permute-start | bytes 2752520 | tf_op jit(solution)/shard_map/ppermute | solution.py:15
  360.1 25.7 %collective-permute-start.20 = (bf16[7,256,256]{1,2,0:T(8,128)(2,1)}, bf16[7,256,256]{1,2,0:T(8,128)(2,1)S(1)}, u32[]{:S(2)}, u32[]{:S(2)}) collective-permute-start(bf16[7,256,256]{1,2,0:T(8,128)(2,1)} %bitcast_dynamic-update-slice_fusion.25), channel_id=1, source_target_pairs={{32,0},{48,16},{64,32},{80,48},{96,64},{112,80},{33,1},{49,17},{65... | collective-permute-start | bytes 2752520 | tf_op jit(solution)/shard_map/ppermute | solution.py:15
  367.2 45.4 %collective-permute-start.8 = (bf16[3,1,768,256]{2,3,1,0:T(8,128)(2,1)}, bf16[3,1,768,256]{2,3,1,0:T(8,128)(2,1)}, u32[]{:S(2)}, u32[]{:S(2)}) collective-permute-start(bf16[3,1,768,256]{2,3,1,0:T(8,128)(2,1)} %pad_maximum_fusion.2), channel_id=1, source_target_pairs={{0,1},{1,2},{2,3},{3,4},{4,5},{5,6},{6,7},{7,8},{8,9},{9,10},{10,1... | collective-permute-start | bytes 3538952 | tf_op jit(solution)/shard_map/ppermute | solution.py:23
  374.4 38.2 %collective-permute-start.9 = (bf16[3,1,768,256]{2,3,1,0:T(8,128)(2,1)}, bf16[3,1,768,256]{2,3,1,0:T(8,128)(2,1)}, u32[]{:S(2)}, u32[]{:S(2)}) collective-permute-start(bf16[3,1,768,256]{2,3,1,0:T(8,128)(2,1)} %pad_maximum_fusion.2), channel_id=1, source_target_pairs={{1,0},{2,1},{3,2},{4,3},{5,4},{6,5},{7,6},{8,7},{9,8},{10,9},{11,1... | collective-permute-start | bytes 3538952 | tf_op jit(solution)/shard_map/ppermute | solution.py:26
  428.5 189.4 %all-reduce.15.cloned.1.call-start = ((), (), s32[]{:S(2)}) async-start(), calls=%async_computation.2 | async-start | bytes 524288 | tf_op jit(solution)/shard_map/psum | solution.py:157
  530.1 234.8 %all-reduce.17.cloned.1.call-start = ((), (), s32[]{:S(2)}) async-start(), calls=%async_computation.3 | async-start | bytes 524288 | tf_op jit(solution)/shard_map/psum | solution.py:159
  622.6 505.5 %all-reduce.19.cloned.1.call-start = ((), (), s32[]{:S(2)}) async-start(), calls=%async_computation.4 | async-start | bytes 1048576 | tf_op jit(solution)/shard_map/psum | solution.py:157
  911.9 52.9 %collective-permute-start.36 = (bf16[7,256,256]{1,2,0:T(8,128)(2,1)}, bf16[7,256,256]{1,2,0:T(8,128)(2,1)}, u32[]{:S(2)}, u32[]{:S(2)}) collective-permute-start(bf16[7,256,256]{1,2,0:T(8,128)(2,1)} %bitcast_dynamic-update-slice_fusion.19), channel_id=1, source_target_pairs={{0,48},{16,64},{32,80},{48,96},{64,112},{1,49},{17,65},{33,81},{49... | collective-permute-start | bytes 2752520 | tf_op jit(solution)/shard_map/ppermute | solution.py:15
  920.2 48.1 %collective-permute-start.37 = (bf16[7,256,256]{1,2,0:T(8,128)(2,1)}, bf16[7,256,256]{1,2,0:T(8,128)(2,1)}, u32[]{:S(2)}, u32[]{:S(2)}) collective-permute-start(bf16[7,256,256]{1,2,0:T(8,128)(2,1)} %bitcast_dynamic-update-slice_fusion.19), channel_id=1, source_target_pairs={{0,32},{16,48},{32,64},{48,80},{64,96},{80,112},{1,33},{17,49},{33... | collective-permute-start | bytes 2752520 | tf_op jit(solution)/shard_map/ppermute | solution.py:15
  922.5 38.0 %collective-permute-start.26 = (bf16[1,1,768,256]{2,3,1,0:T(8,128)(2,1)S(1)}, bf16[1,1,768,256]{2,3,1,0:T(8,128)(2,1)S(1)}, u32[]{:S(2)}, u32[]{:S(2)}) collective-permute-start(bf16[1,1,768,256]{2,3,1,0:T(8,128)(2,1)S(1)} %convert_bitcast_fusion), channel_id=1, source_target_pairs={{0,16},{16,32},{32,48},{48,64},{64,80},{80,96},{96,112},{1,17},{17... | collective-permute-start | bytes 1179656 | tf_op jit(solution)/shard_map/ppermute | solution.py:23
  924.4 38.0 %collective-permute-start.27 = (bf16[1,1,768,256]{2,3,1,0:T(8,128)(2,1)S(1)}, bf16[1,1,768,256]{2,3,1,0:T(8,128)(2,1)S(1)}, u32[]{:S(2)}, u32[]{:S(2)}) collective-permute-start(bf16[1,1,768,256]{2,3,1,0:T(8,128)(2,1)S(1)} %convert_bitcast_fusion), channel_id=1, source_target_pairs={{16,0},{32,16},{48,32},{64,48},{80,64},{96,80},{112,96},{17,1},{33... | collective-permute-start | bytes 1179656 | tf_op jit(solution)/shard_map/ppermute | solution.py:26
  926.8 48.7 %collective-permute-start.38 = (bf16[7,256,256]{1,2,0:T(8,128)(2,1)}, bf16[7,256,256]{1,2,0:T(8,128)(2,1)}, u32[]{:S(2)}, u32[]{:S(2)}) collective-permute-start(bf16[7,256,256]{1,2,0:T(8,128)(2,1)} %bitcast_dynamic-update-slice_fusion.19), channel_id=1, source_target_pairs={{0,16},{16,32},{32,48},{48,64},{64,80},{80,96},{96,112},{1,17},{17... | collective-permute-start | bytes 2752520 | tf_op jit(solution)/shard_map/ppermute | solution.py:15
  962.4 25.7 %collective-permute-start.40 = (bf16[7,256,256]{1,2,0:T(8,128)(2,1)}, bf16[7,256,256]{1,2,0:T(8,128)(2,1)S(1)}, u32[]{:S(2)}, u32[]{:S(2)}) collective-permute-start(bf16[7,256,256]{1,2,0:T(8,128)(2,1)} %bitcast_dynamic-update-slice_fusion.19), channel_id=1, source_target_pairs={{32,0},{48,16},{64,32},{80,48},{96,64},{112,80},{33,1},{49,17},{65... | collective-permute-start | bytes 2752520 | tf_op jit(solution)/shard_map/ppermute | solution.py:15
  964.8 24.2 %collective-permute-start.41 = (bf16[7,256,256]{1,2,0:T(8,128)(2,1)}, bf16[7,256,256]{1,2,0:T(8,128)(2,1)S(1)}, u32[]{:S(2)}, u32[]{:S(2)}) collective-permute-start(bf16[7,256,256]{1,2,0:T(8,128)(2,1)} %bitcast_dynamic-update-slice_fusion.19), channel_id=1, source_target_pairs={{48,0},{64,16},{80,32},{96,48},{112,64},{49,1},{65,17},{81,33},{97... | collective-permute-start | bytes 2752520 | tf_op jit(solution)/shard_map/ppermute | solution.py:15
  968.3 44.0 %collective-permute-start.28 = (bf16[3,1,768,256]{2,3,1,0:T(8,128)(2,1)}, bf16[3,1,768,256]{2,3,1,0:T(8,128)(2,1)}, u32[]{:S(2)}, u32[]{:S(2)}) collective-permute-start(bf16[3,1,768,256]{2,3,1,0:T(8,128)(2,1)} %pad_maximum_fusion.3), channel_id=1, source_target_pairs={{0,1},{1,2},{2,3},{3,4},{4,5},{5,6},{6,7},{7,8},{8,9},{9,10},{10,1... | collective-permute-start | bytes 3538952 | tf_op jit(solution)/shard_map/ppermute | solution.py:23
  975.6 36.7 %collective-permute-start.29 = (bf16[3,1,768,256]{2,3,1,0:T(8,128)(2,1)}, bf16[3,1,768,256]{2,3,1,0:T(8,128)(2,1)}, u32[]{:S(2)}, u32[]{:S(2)}) collective-permute-start(bf16[3,1,768,256]{2,3,1,0:T(8,128)(2,1)} %pad_maximum_fusion.3), channel_id=1, source_target_pairs={{1,0},{2,1},{3,2},{4,3},{5,4},{6,5},{7,6},{8,7},{9,8},{10,9},{11,1... | collective-permute-start | bytes 3538952 | tf_op jit(solution)/shard_map/ppermute | solution.py:26
  1027.6 189.1 %all-reduce.21.cloned.1.call-start = ((), (), s32[]{:S(2)}) async-start(), calls=%async_computation.5 | async-start | bytes 1048576 | tf_op jit(solution)/shard_map/psum | solution.py:157
  1128.1 235.6 %all-reduce.23.cloned.1.call-start = ((), (), s32[]{:S(2)}) async-start(), calls=%async_computation.6 | async-start | bytes 524288 | tf_op jit(solution)/shard_map/psum | solution.py:159
  (70 other events, 1762.6 us)
Sparse Core Ops, SparseCore 0:
  12.1 144.7 all-reduce.10
  428.6 101.4 all-reduce.12
  533.6 84.2 all-reduce.14
  622.8 142.1 all-reduce.16
  1027.7 100.3 all-reduce.18
  1131.5 85.1 all-reduce.20
  1221.5 142.1 all-reduce.22
